TPU v7x, 32 devices: a whole 2x2x4 slice. The times are simulated.
32 devices in a mesh: head: 2 (over x), blk: 16 (over z, y, core).
Axes of the slice: x: 2, y: 2, z: 4, core: 2. Of those that a mesh axis runs over, the one named last changes fastest.
Arguments:
- hidden_in: bfloat16 [512, 2048], P('blk'), may hold values from -6 to 6
- attn_gain: float32 [2048], replicated, may hold values from 0.25 to 1.75
- w_query: bfloat16 [1536, 2048], P('head'), may hold values from -0.125 to 0.125
- w_latent: bfloat16 [576, 2048], P('head'), may hold values from -0.125 to 0.125
- kv_gain: float32 [512], replicated, may hold values from 0.25 to 1.75
- w_key_up: bfloat16 [512, 1024], P(None, 'head'), may hold values from -0.25 to 0.25
- w_value_up: bfloat16 [512, 1024], P(None, 'head'), may hold values from -0.25 to 0.25
- w_out: bfloat16 [1024, 2048], P('head'), may hold values from -0.1875 to 0.1875
- cache_rows: bfloat16 [6144, 576], P('blk'), may hold values from -6 to 6
- slot_request: int32 [48], P('blk'), may hold values from -1 to 15, as said below
- slot_block: int32 [48], P('blk'), may hold values from 0 to 16
- lengths: int32 [16], replicated, may hold values from 1 to 2176, as said below
- parents: int32 [16, 32], P('blk'), may hold values from -1 to 30, as said below
- accepted: int32 [16, 8], P('blk'), may hold values from 0 to 28, as said below
- new_slots: int32 [16, 8], P('blk'), may hold values from 0 to 255, as said below
- moe_gain: float32 [2048], replicated, may hold values from 0.25 to 1.75
- routes: int32 [512, 6], P('blk'), may hold values from 0 to 15, all different within a row; in each aligned block of 32 rows (0 to 31, 32 to 63, ...) at most 24 rows name the same one
- route_logits: float32 [512, 6], P('blk'), may hold values from -8 to 8
- w_gate: bfloat16 [16, 1408, 2048], P('blk', 'head'), may hold values from -0.125 to 0.125
- w_up: bfloat16 [16, 1408, 2048], P('blk', 'head'), may hold values from -0.125 to 0.125
- w_down: bfloat16 [16, 1408, 2048], P('blk', 'head'), may hold values from -0.15625 to 0.15625
Outputs:
- layer_out: bfloat16 [512, 2048], P('blk')
- new_rows: bfloat16 [256, 576], P('blk')
Inputs may be any that keep to these rules, and one draw needn't show every extreme that they name: A pool slot holds block slot_block of request slot_request or is free (-1); each request's blocks are distinct slots. Request r holds exactly ceil(lengths[r] / 128) pool blocks, numbered 0 upwards; one request holds 17 full blocks. `parents`: entry 0 of each request is -1 (the root); entry i names one of the tokens i - 4 .. i - 1. `accepted`: the first 8 tokens of a path from the root down the request's tree, root first. `new_slots`: all distinct. `routes`: within the 32 rows of one index of blk no expert is named more than 24 times.
All inputs are finite; a program needn't handle non-finite values.
Results may differ from a plain program's by a relative error of at most 0.0075.
Values may be sent and summed in bfloat16 or wider, within the bound.
No kernel may reach another device: no remote copies, remote signals or barrier semaphores. Data moves between devices by JAX's collectives and lax.ppermute only.
A program may use at most 128 MiB of HBM per device.

v0:
```python
import jax
import jax.numpy as jnp
from jax import lax
from jax.sharding import PartitionSpec as P

NOPE = 128
ROPE = 64
VDIM = 128
RANK = 512
NEW_DEV = 16
EPSILON = 1e-06
ROUTE_SCALE = 2.446
ROPE_BASE = 50000.0


def rms_scale(values, gain):
    values = values.astype(jnp.float32)
    mean_square = jnp.mean(values * values, axis=-1, keepdims=True)
    return values * lax.rsqrt(mean_square + EPSILON) * gain


def rotate(values, positions):
    width = values.shape[-1]
    half = width // 2
    freqs = ROPE_BASE ** (-2.0 * jnp.arange(half, dtype=jnp.float32) / width)
    angles = positions[:, None] * freqs[None, :]
    cosine = jnp.cos(angles)[:, None, :]
    sine = jnp.sin(angles)[:, None, :]
    first = values[..., :half]
    second = values[..., half:]
    return jnp.concatenate(
        [first * cosine - second * sine, second * cosine + first * sine], axis=-1
    )


def ancestry(parents):
    count = parents.shape[-1]
    nodes = jnp.arange(count, dtype=jnp.int32)
    reach = (parents[:, :, None] == nodes[None, None, :]).astype(jnp.float32) + jnp.eye(
        count, dtype=jnp.float32
    )[None]
    for level in range(count.bit_length()):
        reach = jnp.minimum(
            jnp.einsum("rij,rjk->rik", reach, reach, precision=lax.Precision.HIGHEST), 1.0
        )
    return reach


def expand(rows, key_up, value_up):
    count = rows.shape[0]
    heads_here = key_up.shape[1] // NOPE
    key_nope = (
        jnp.dot(rows[:, :RANK], key_up, preferred_element_type=jnp.float32)
        .astype(jnp.bfloat16)
        .reshape(count, heads_here, NOPE)
    )
    values = (
        jnp.dot(rows[:, :RANK], value_up, preferred_element_type=jnp.float32)
        .astype(jnp.bfloat16)
        .reshape(count, heads_here, VDIM)
    )
    shared = jnp.broadcast_to(rows[:, None, RANK:], (count, heads_here, ROPE))
    return (jnp.concatenate([key_nope, shared], axis=-1), values)


def project_rows(left, weight_rows):
    return lax.dot_general(
        left, weight_rows, (((1,), (1,)), ((), ())), preferred_element_type=jnp.float32
    )


def shards(
    hidden_in,
    attn_gain,
    w_query,
    w_latent,
    kv_gain,
    w_key_up,
    w_value_up,
    w_out,
    cache_rows,
    slot_request,
    slot_block,
    lengths,
    parents,
    accepted,
    new_slots,
    moe_gain,
    routes,
    route_logits,
    w_gate,
    w_up,
    w_down,
):
    block_count = lax.axis_size("blk")
    block_index = lax.axis_index("blk")
    tok_rows = hidden_in.shape[0]
    model_width = hidden_in.shape[1]
    req_local = parents.shape[0]
    draft_len = parents.shape[1]
    requests = lengths.shape[0]
    heads_here = w_key_up.shape[1] // NOPE
    top_count = routes.shape[1]
    scale = (NOPE + ROPE) ** (-0.5)
    normed = rms_scale(hidden_in, attn_gain).astype(jnp.bfloat16)
    reach = ancestry(parents)
    depth = jnp.sum(reach, axis=-1) - 1.0
    local_lengths = lax.dynamic_slice_in_dim(lengths, block_index * req_local, req_local, 0)
    positions = (local_lengths.astype(jnp.float32)[:, None] + depth).reshape(tok_rows)
    query_full = project_rows(normed, w_query).reshape(tok_rows, heads_here, NOPE + ROPE)
    queries = jnp.concatenate(
        [query_full[..., :NOPE], rotate(query_full[..., NOPE:], positions)], axis=-1
    ).astype(jnp.bfloat16)
    latent_part = project_rows(normed, w_latent)
    compressed = lax.all_gather(latent_part, "head", axis=1, tiled=True)
    draft_rows = jnp.concatenate(
        [
            rms_scale(compressed[:, :RANK], kv_gain),
            rotate(compressed[:, None, RANK:], positions)[:, 0],
        ],
        axis=-1,
    ).astype(jnp.bfloat16)
    chosen = (jnp.arange(req_local, dtype=jnp.int32)[:, None] * draft_len + accepted).reshape(-1)
    all_queries, all_chosen, all_targets = (
        lax.all_gather(
            queries.reshape(tok_rows, heads_here * (NOPE + ROPE)), "blk", axis=0, tiled=True
        ),
        lax.all_gather(draft_rows[chosen], "blk", axis=0, tiled=True),
        lax.all_gather(new_slots.reshape(-1), "blk", axis=0, tiled=True),
    )
    local_target = all_targets - block_index * NEW_DEV
    local_target = jnp.where((local_target >= 0) & (local_target < NEW_DEV), local_target, NEW_DEV)
    new_rows = (
        jnp.zeros((NEW_DEV, RANK + ROPE), jnp.bfloat16)
        .at[local_target]
        .set(all_chosen, mode="drop")
    )
    cache_keys, cache_values = expand(cache_rows, w_key_up, w_value_up)
    slot_count = slot_request.shape[0]
    block_len = cache_rows.shape[0] // slot_count
    owner = jnp.maximum(slot_request, 0)
    slot_queries = all_queries.reshape(requests, draft_len, heads_here, NOPE + ROPE)[owner]
    key_blocks = cache_keys.reshape(slot_count, block_len, heads_here, NOPE + ROPE)
    value_blocks = cache_values.reshape(slot_count, block_len, heads_here, VDIM)
    key_place = slot_block[:, None] * block_len + jnp.arange(block_len, dtype=jnp.int32)[None, :]
    live = (key_place < lengths[owner][:, None]) & (slot_request >= 0)[:, None]
    scores = (
        jnp.einsum("sqhd,skhd->sqhk", slot_queries, key_blocks, preferred_element_type=jnp.float32)
        * scale
    )
    weights = jnp.where(live[:, None, None, :], jnp.exp(scores), 0.0)
    slot_denom = jnp.sum(weights, axis=-1)
    slot_numer = jnp.einsum(
        "sqhk,skhv->sqhv",
        weights.astype(jnp.bfloat16),
        value_blocks,
        preferred_element_type=jnp.float32,
    )
    selector = (slot_request[None, :] == jnp.arange(requests, dtype=jnp.int32)[:, None]).astype(
        jnp.float32
    )
    numer_out = jnp.einsum(
        "rs,sqhv->rqhv", selector, slot_numer, precision=lax.Precision.HIGHEST
    ).reshape(requests * draft_len, heads_here * VDIM)
    denom_out = jnp.einsum(
        "rs,sqh->rqh", selector, slot_denom, precision=lax.Precision.HIGHEST
    ).reshape(requests * draft_len, heads_here)
    numer_in, denom_in = (
        lax.all_to_all(numer_out, "blk", split_axis=0, concat_axis=0, tiled=True),
        lax.all_to_all(denom_out, "blk", split_axis=0, concat_axis=0, tiled=True),
    )
    numer_far = numer_in.reshape(block_count, tok_rows, heads_here * VDIM).sum(axis=0)
    denom_far = denom_in.reshape(block_count, tok_rows, heads_here).sum(axis=0)
    draft_keys, draft_values = expand(draft_rows, w_key_up, w_value_up)
    own_keys = draft_keys.reshape(req_local, draft_len, heads_here, NOPE + ROPE)
    own_values = draft_values.reshape(req_local, draft_len, heads_here, VDIM)
    own_queries = queries.reshape(req_local, draft_len, heads_here, NOPE + ROPE)
    own_scores = (
        jnp.einsum("rqhd,rkhd->rqhk", own_queries, own_keys, preferred_element_type=jnp.float32)
        * scale
    )
    own_weights = jnp.where((reach > 0.5)[:, :, None, :], jnp.exp(own_scores), 0.0)
    denom = jnp.sum(own_weights, axis=-1).reshape(tok_rows, heads_here) + denom_far
    numer = jnp.einsum(
        "rqhk,rkhv->rqhv",
        own_weights.astype(jnp.bfloat16),
        own_values,
        preferred_element_type=jnp.float32,
    ).reshape(tok_rows, heads_here, VDIM)
    numer = numer + numer_far.reshape(tok_rows, heads_here, VDIM)
    attended = (numer / denom[..., None]).astype(jnp.bfloat16).reshape(tok_rows, heads_here * VDIM)
    attn_sum = lax.psum(jnp.dot(attended, w_out, preferred_element_type=jnp.float32), "head")
    resid = (hidden_in.astype(jnp.float32) + attn_sum).astype(jnp.bfloat16)
    moe_in = rms_scale(resid, moe_gain).astype(jnp.bfloat16)
    sigma = jax.nn.sigmoid(route_logits)
    route_weight = (ROUTE_SCALE * sigma / jnp.sum(sigma, axis=-1, keepdims=True)).reshape(-1)
    local_experts = w_gate.shape[0]
    expert_total = local_experts * block_count
    capacity = 2 * tok_rows * top_count // expert_total
    flat_routes = routes.reshape(-1)
    onehot = (flat_routes[:, None] == jnp.arange(expert_total, dtype=jnp.int32)[None, :]).astype(
        jnp.int32
    )
    rank = jnp.sum((jnp.cumsum(onehot, axis=0) - onehot) * onehot, axis=-1)
    slot_ids = flat_routes * capacity + rank
    source_rows = (
        jnp.full((expert_total * capacity,), tok_rows, jnp.int32)
        .at[slot_ids]
        .set(jnp.arange(tok_rows * top_count, dtype=jnp.int32) // top_count)
    )
    moe_pad = jnp.concatenate([moe_in, jnp.zeros((1, model_width), jnp.bfloat16)], axis=0)
    send_rows = moe_pad[source_rows]
    received = lax.all_to_all(send_rows, "blk", split_axis=0, concat_axis=0, tiled=True)
    grouped = received.reshape(block_count, local_experts, capacity, model_width)
    gate_val = jnp.einsum("sjcd,jfd->sjcf", grouped, w_gate, preferred_element_type=jnp.float32)
    up_val = jnp.einsum("sjcd,jfd->sjcf", grouped, w_up, preferred_element_type=jnp.float32)
    act = (jax.nn.silu(gate_val) * up_val).astype(jnp.bfloat16)
    expert_out = jnp.einsum(
        "sjcf,jfd->sjcd", act, w_down, preferred_element_type=jnp.float32
    ).reshape(block_count * local_experts * capacity, model_width)
    back = lax.all_to_all(expert_out, "blk", split_axis=0, concat_axis=0, tiled=True)
    routed_part = (
        (back[slot_ids] * route_weight[:, None])
        .reshape(tok_rows, top_count, model_width)
        .sum(axis=1)
    )
    routed = lax.psum(routed_part, "head")
    layer_out = (resid.astype(jnp.float32) + routed).astype(jnp.bfloat16)
    return (layer_out, new_rows)


def solution(mesh):
    return jax.shard_map(
        shards,
        mesh=mesh,
        in_specs=(
            P("blk", None),
            P(),
            P("head", None),
            P("head", None),
            P(),
            P(None, "head"),
            P(None, "head"),
            P("head", None),
            P("blk", None),
            P("blk"),
            P("blk"),
            P(),
            P("blk", None),
            P("blk", None),
            P("blk", None),
            P(),
            P("blk", None),
            P("blk", None),
            P("blk", "head", None),
            P("blk", "head", None),
            P("blk", "head", None),
        ),
        out_specs=(P("blk", None), P("blk", None)),
        check_vma=False,
    )
```

profile of v0, /device:TPU:0, one launch (start us, length us, event | category | flops | bytes accessed | tf_op | source)
XLA Modules:
  0.0 325.3 jit_solution(3864422452794586233)
XLA Ops:
  10.8 2.0 fusion.53
  17.2 1.4 copy_bitcast_fusion
  20.8 2.3 convolution_convert_fusion
  25.1 27.0 %all_gather.13 = bf16[512,768]{1,0:T(8,128)(2,1)} all-gather(bf16[32,768]{1,0:T(8,128)(2,1)} %convert_element_type.121), channel_id=1, replica_groups=mesh['head'=2,'blk'=16] {'blk'}, dimensions={0}, use_global_device_ids=true | all-gather | bytes 835584 | tf_op jit(solution)/shard_map/all_gather | solution.py:125
  52.2 3.4 %reshape.528 = bf16[16,32,4,192]{3,2,1,0:T(4,128)(2,1)} reshape(bf16[512,768]{1,0:T(8,128)(2,1)} %all_gather.13) | data formatting | bytes 1572864 | tf_op jit(solution)/shard_map/reshape | solution.py:142
  55.6 2.5 copy.84
  58.1 1.9 gather_fusion.1
  60.8 2.0 fusion.95
  63.8 3.5 %all-to-all-start.1 = ((f32[16,1,128]{2,1,0:T(1,128)}), f32[16,1,128]{2,1,0:T(1,128)S(1)}, u32[]{:S(2)}, u32[]{:S(2)}) async-start(f32[16,1,128]{2,1,0:T(1,128)} %reshape.622), calls=%async_computation.1 | async-start | bytes 16384 | tf_op jit(solution)/shard_map/all_to_all | solution.py:170
  69.5 1.7 convolution_bitcast_fusion.2
  71.2 4.8 %all-gather.2 = f32[2,288,32]{1,2,0:T(8,128)S(1)} all-gather(f32[1,288,32]{1,2,0:T(8,128)S(1)} %convolution_bitcast_fusion.2), channel_id=1, replica_groups=mesh['head'=2,'blk'=16] {'head'}, dimensions={0}, use_global_device_ids=true | all-gather | bytes 110592 | tf_op jit(solution)/shard_map/all_gather | solution.py:115
  76.3 2.3 convolution_convert_fusion.1
  78.6 1.9 reshape_reshape.4
  81.7 1.7 fusion.46
  85.1 2.7 copy.87
  87.8 2.6 all_to_all.22
  90.5 6.2 %all-to-all-start = ((f32[16,32,512]{2,1,0:T(8,128)}), f32[16,32,512]{2,1,0:T(8,128)}, u32[]{:S(2)}, u32[]{:S(2)}) async-start(f32[16,32,512]{2,1,0:T(8,128)} %all_to_all.22), calls=%async_computation | async-start | bytes 2097152 | tf_op jit(solution)/shard_map/all_to_all | solution.py:169
  105.3 14.4 %all-to-all-done = f32[16,32,512]{2,1,0:T(8,128)} async-done(((f32[16,32,512]{2,1,0:T(8,128)}), f32[16,32,512]{2,1,0:T(8,128)}, u32[]{:S(2)}, u32[]{:S(2)}) %all-to-all-start) | async-done | bytes 1048608 | tf_op jit(solution)/shard_map/all_to_all | solution.py:169
  121.1 2.8 fusion.56
  123.9 25.5 %all-reduce.6.cloned.1.call-done = f32[32,2048]{1,0:T(8,128)} async-done(((f32[32,2048]{1,0:T(8,128)}), f32[32,2048]{1,0:T(8,128)}) %all-reduce.6.cloned.1.call-update) | async-done | bytes 262160 | tf_op jit(solution)/shard_map/psum | solution.py:192
  150.6 3.1 gather_fusion.2
  153.8 42.0 %all_to_all.33 = bf16[16,24,2048]{2,1,0:T(8,128)(2,1)S(1)} all-to-all(bf16[16,24,2048]{2,1,0:T(8,128)(2,1)} %bitcast.171), channel_id=1, replica_groups=mesh['head'=2,'blk'=16] {'blk'}, dimensions={0} | all-to-all | bytes 3145728 | tf_op jit(solution)/shard_map/all_to_all | solution.py:213
  196.9 2.6 fusion.6
  199.4 8.3 %fusion = f32[16,24,2048]{2,1,0:T(8,128)} fusion(bf16[1,704,2048]{2,1,0:T(8,128)(2,1)} %param.41, bf16[16,24,2048]{2,1,0:T(8,128)(2,1)} %copy-done.3, bf16[1,704,2048]{2,1,0:T(8,128)(2,1)} %param.40, f32[16,1,24,704]{3,2,0,1:T(8,128)} %fusion.6), kind=kOutput, calls=%fused_computation.7 | convolution fusion | flops 2216214528 | bytes 11567104 | tf_op jit(solution)/shard_map/sjcf,jfd->sjcd/dot_general | solution.py:218
  207.7 5.2 %all-to-all-start.3 = ((f32[16,24,2048]{2,1,0:T(8,128)}), f32[16,24,2048]{2,1,0:T(8,128)}, u32[]{:S(2)}, u32[]{:S(2)}) async-start(f32[16,24,2048]{2,1,0:T(8,128)} %fusion), calls=%async_computation.3 | async-start | bytes 6291456 | tf_op jit(solution)/shard_map/all_to_all | solution.py:221
  215.2 69.5 %all-reduce.2 = s32[128]{0:T(128)S(1)} all-reduce(s32[128]{0:T(128)S(1)} %bitcast_dynamic-update-slice_fusion), channel_id=2, replica_groups=mesh['head'=2,'blk'=16] {'blk'}, use_global_device_ids=true, to_apply=%add.2 | all-reduce | flops 128 | bytes 1024
  284.7 4.9 %gather_fusion.3 = f32[192,2048]{1,0:T(8,128)} fusion(f32[384,2048]{1,0:T(8,128)} %bitcast.37, s32[1024]{0:T(1024)S(1)} %pad_clamp_fusion.1), kind=kCustom, calls=%fused_computation.3 | custom fusion | bytes 3146496 | tf_op jit(solution)/shard_map/gather | solution.py:223
  289.6 2.7 gather.21
  292.3 3.1 multiply_reduce_fusion
  295.3 19.8 %all-gather.1 = bf16[128,576]{1,0:T(8,128)(2,1)S(1)} all-gather(bf16[8,576]{1,0:T(8,128)(2,1)S(1)} %gather_fusion.4), channel_id=3, replica_groups=mesh['head'=2,'blk'=16] {'blk'}, dimensions={0}, use_global_device_ids=true | all-gather | bytes 156672 | tf_op jit(solution)/shard_map/all_gather | solution.py:128
  315.2 1.6 scatter_custom_fusion.1
  316.8 1.6 fusion.45
  (164 shorter events, 32.5 us)
Async XLA Ops:
  7.2 3.6 %copy-start = (bf16[768,2048]{1,0:T(8,128)(2,1)S(1)}, bf16[768,2048]{1,0:T(8,128)(2,1)}, u32[]{:S(2)}) copy-start(bf16[768,2048]{1,0:T(8,128)(2,1)} %param.23) | copy-start | bytes 9437188
  10.8 3.5 %copy-start.28 = (s32[3]{0:T(128)S(1)}, s32[3]{0:T(128)}, u32[]{:S(2)}) copy-start(s32[3]{0:T(128)} %param.31) | copy-start | bytes 40
  10.8 5.3 %copy-start.26 = (s32[1,32]{1,0:T(1,128)S(1)}, s32[1,32]{1,0:T(1,128)}, u32[]{:S(2)}) copy-start(s32[1,32]{1,0:T(1,128)} %param.33) | copy-start | bytes 388
  14.9 4.4 %copy-start.15 = (s32[1024]{0:T(1024)}, s32[1024]{0:T(1024)S(1)}, u32[]{:S(2)}) copy-start(s32[1024]{0:T(1024)S(1)} %pad_clamp_fusion.3) | copy-start | bytes 12292
  55.6 4.4 %copy-start.22 = (s32[3]{0:T(128)S(1)}, s32[3]{0:T(128)}, u32[]{:S(2)}) copy-start(s32[3]{0:T(128)} %gather_fusion) | copy-start | bytes 40
  55.6 5.2 %copy-start.6 = (bf16[3,128,64]{1,2,0:T(8,128)(2,1)S(1)}, bf16[3,128,64]{1,2,0:T(8,128)(2,1)}, u32[]{:S(2)}) copy-start(bf16[3,128,64]{1,2,0:T(8,128)(2,1)} %copy_bitcast_fusion) | copy-start | bytes 147460
  55.6 7.2 %copy-start.24 = (s32[3]{0:T(128)S(1)}, s32[3]{0:T(128)}, u32[]{:S(2)}) copy-start(s32[3]{0:T(128)} %param.30) | copy-start | bytes 40
  58.1 11.4 %copy-start.2 = (bf16[32,2048]{1,0:T(8,128)(2,1)S(1)}, bf16[32,2048]{1,0:T(8,128)(2,1)}, u32[]{:S(2)}) copy-start(bf16[32,2048]{1,0:T(8,128)(2,1)} %param.21) | copy-start | bytes 393220
  58.1 11.4 %copy-start.10 = (f32[2048]{0:T(1024)S(1)}, f32[2048]{0:T(1024)}, u32[]{:S(2)}) copy-start(f32[2048]{0:T(1024)} %param.22) | copy-start | bytes 24580
  63.8 26.7 %all-to-all-start.1 = ((f32[16,1,128]{2,1,0:T(1,128)}), f32[16,1,128]{2,1,0:T(1,128)S(1)}, u32[]{:S(2)}, u32[]{:S(2)}) async-start(f32[16,1,128]{2,1,0:T(1,128)} %reshape.622), calls=%async_computation.1 | async-start | bytes 16384 | tf_op jit(solution)/shard_map/all_to_all | solution.py:170
  68.8 9.8 %copy-start.13 = (s32[192]{0:T(256)}, s32[192]{0:T(256)S(1)}, u32[]{:S(2)}) copy-start(s32[192]{0:T(256)S(1)} %eq.99) | copy-start | bytes 2308
  76.2 4.3 %copy-start.7 = (bf16[3,32,4,128]{3,1,2,0:T(8,128)(2,1)S(1)}, bf16[3,32,4,128]{3,1,2,0:T(8,128)(2,1)}, u32[]{:S(2)}) copy-start(bf16[3,32,4,128]{3,1,2,0:T(8,128)(2,1)} %get-tuple-element.17) | copy-start | bytes 294916
  76.2 5.5 %copy-start.25 = (s32[3]{0:T(128)S(1)}, s32[3]{0:T(128)}, u32[]{:S(2)}) copy-start(s32[3]{0:T(128)} %param.30) | copy-start | bytes 40
  78.6 4.8 %copy-start.21 = (f32[512]{0:T(512)S(1)}, f32[512]{0:T(512)}, u32[]{:S(2)}) copy-start(f32[512]{0:T(512)} %param.25) | copy-start | bytes 6148
  85.1 5.3 %copy-start.20 = (s32[16,3]{0,1:T(4,128)}, s32[16,3]{0,1:T(4,128)S(1)}, u32[]{:S(2)}) copy-start(s32[16,3]{0,1:T(4,128)S(1)} %reduce-window.9) | copy-start | bytes 580
  90.4 7.5 %copy-start.17 = (f32[32]{0:T(128)S(1)}, f32[32]{0:T(128)}, u32[]{:S(2)}) copy-start(f32[32]{0:T(128)} %copy-done.16) | copy-start | bytes 388
  90.5 7.5 %copy-start.19 = (f32[32]{0:T(128)S(1)}, f32[32]{0:T(128)}, u32[]{:S(2)}) copy-start(f32[32]{0:T(128)} %copy-done.18) | copy-start | bytes 388
  90.5 9.0 %copy-start.5 = (bf16[32,4,192]{2,0,1:T(8,128)(2,1)S(1)}, bf16[32,4,192]{2,0,1:T(8,128)(2,1)}, u32[]{:S(2)}) copy-start(bf16[32,4,192]{2,0,1:T(8,128)(2,1)} %copy-done.4) | copy-start | bytes 147460
  90.5 7.8 %copy-start.11 = (f32[16,1,128]{2,1,0:T(1,128)}, f32[16,1,128]{2,1,0:T(1,128)S(1)}, u32[]{:S(2)}) copy-start(f32[16,1,128]{2,1,0:T(1,128)S(1)} %all-to-all-done.1) | copy-start | bytes 24580
  90.5 29.2 %all-to-all-start = ((f32[16,32,512]{2,1,0:T(8,128)}), f32[16,32,512]{2,1,0:T(8,128)}, u32[]{:S(2)}, u32[]{:S(2)}) async-start(f32[16,32,512]{2,1,0:T(8,128)} %all_to_all.22), calls=%async_computation | async-start | bytes 2097152 | tf_op jit(solution)/shard_map/all_to_all | solution.py:169
  96.7 52.7 %all-reduce.6.cloned.1.call-start = ((), (), s32[]{:S(2)}) async-start(), calls=%async_computation.4 | async-start | bytes 524288 | tf_op jit(solution)/shard_map/psum | solution.py:192
  96.7 3.9 %slice-start = ((s32[16,3]{0,1:T(4,128)}), s32[16,2]{0,1:T(2,128)S(1)}, s32[]{:S(2)}) async-start(s32[16,3]{0,1:T(4,128)} %copy-done.20), calls=%async_computation.6 | async-start | bytes 2048 | tf_op jit(solution)/shard_map/slice.1
  98.2 25.6 %copy-start.8 = (bf16[32,64]{1,0:T(8,128)(2,1)}, bf16[32,64]{1,0:T(8,128)(2,1)S(1)}, u32[]{:S(2)}) copy-start(bf16[32,64]{1,0:T(8,128)(2,1)S(1)} %maximum_bitcast_fusion) | copy-start | bytes 12292
  121.0 29.4 %copy-start.14 = (f32[2048]{0:T(1024)S(1)}, f32[2048]{0:T(1024)}, u32[]{:S(2)}) copy-start(f32[2048]{0:T(1024)} %param.36) | copy-start | bytes 24580
  153.8 43.1 %copy-start.27 = (bf16[1,704,2048]{2,1,0:T(8,128)(2,1)S(1)}, bf16[1,704,2048]{2,1,0:T(8,128)(2,1)}, u32[]{:S(2)}) copy-start(bf16[1,704,2048]{2,1,0:T(8,128)(2,1)} %param.39) | copy-start | bytes 8650756
  207.7 5.3 %copy-start.12 = (f32[32,6]{0,1:T(8,128)S(1)}, f32[32,6]{0,1:T(8,128)}, u32[]{:S(2)}) copy-start(f32[32,6]{0,1:T(8,128)} %param.38) | copy-start | bytes 2308
  207.7 5.4 %copy-start.31 = (u32[32]{0:T(128)S(1)}, u32[32]{0:T(128)}, u32[]{:S(2)}) copy-start(u32[32]{0:T(128)} %constant.93) | copy-start | bytes 388
  207.7 6.7 %copy-start.29 = (s32[1,8]{1,0:T(1,128)S(1)}, s32[1,8]{1,0:T(1,128)}, u32[]{:S(2)}) copy-start(s32[1,8]{1,0:T(1,128)} %param.34) | copy-start | bytes 100
  207.7 6.7 %copy-start.9 = (bf16[32,64]{1,0:T(8,128)(2,1)S(1)}, bf16[32,64]{1,0:T(8,128)(2,1)}, u32[]{:S(2)}) copy-start(bf16[32,64]{1,0:T(8,128)(2,1)} %copy-done.8) | copy-start | bytes 12292
  207.7 7.3 %copy-start.30 = (s32[1,8]{1,0:T(1,128)S(1)}, s32[1,8]{1,0:T(1,128)}, u32[]{:S(2)}) copy-start(s32[1,8]{1,0:T(1,128)} %param.35) | copy-start | bytes 100
  207.7 77.0 %all-to-all-start.3 = ((f32[16,24,2048]{2,1,0:T(8,128)}), f32[16,24,2048]{2,1,0:T(8,128)}, u32[]{:S(2)}, u32[]{:S(2)}) async-start(f32[16,24,2048]{2,1,0:T(8,128)} %fusion), calls=%async_computation.3 | async-start | bytes 6291456 | tf_op jit(solution)/shard_map/all_to_all | solution.py:221
  213.0 103.8 %all-reduce.8.cloned.1.call-start = ((), (), s32[]{:S(2)}) async-start(), calls=%async_computation.5 | async-start | bytes 524288 | tf_op jit(solution)/shard_map/psum | solution.py:227
  (6 other events, 5.8 us)
Sparse Core Ops, SparseCore 0:
  124.0 25.3 all-reduce.5
  295.5 21.2 all-reduce.7
where the time goes:
time: 327 us; the launch traced here: 325 us
  blocking collectives  163 us (50%)
  local copies, waits for them, and re-layouts  43.3 us (13%)
  waiting for transfers between devices  39.9 us (12%)
  matrix products  31.6 us (10%)
  other arithmetic  16.5 us (5%)
  between operations  15.9 us (5%)
  starting transfers between devices  14.9 us (5%)
    unnamed x1, blocking collectives  69.5 us
    all_to_all x1, blocking collectives, shards(): lax.all_to_all(send_rows, 'blk', split_axis=0, concat_axis=0, tiled=True)  42 us
    all_gather x1, blocking collectives, shards(): lax.all_gather(queries.reshape(tok_rows, heads_here * (NOPE + ROPE)), 'bl...  27 us
    psum x1, waiting for transfers between devices, shards(): lax.psum(jnp.dot(attended, w_out, preferred_element_type=jnp.float32), 'h...  25.5 us
    all_gather x1, blocking collectives, shards(): lax.all_gather(draft_rows[chosen], 'blk', axis=0, tiled=True)  19.8 us
    all_to_all x1, waiting for transfers between devices, shards(): lax.all_to_all(numer_out, 'blk', split_axis=0, concat_axis=0, tiled=True)  14.4 us
    dot_general x1, matrix products, shards(): jnp.einsum('sjcf,jfd->sjcd', act, w_down, preferred_element_type=jnp.floa...  8.28 us
    gather x2, local copies, waits for them, and re-layouts, shards(): back[slot_ids] * route_weight[:, None]  7.57 us
  transfers between devices with their start and end apart: 5, of which 2 were waited for; matrix products, arithmetic and copies ran while one was open for 8% of the time, Pallas kernels for 0%

commit v1 on v0

--- a/solution.py
+++ b/solution.py
@@ -189,7 +189,9 @@
     ).reshape(tok_rows, heads_here, VDIM)
     numer = numer + numer_far.reshape(tok_rows, heads_here, VDIM)
     attended = (numer / denom[..., None]).astype(jnp.bfloat16).reshape(tok_rows, heads_here * VDIM)
-    attn_sum = lax.psum(jnp.dot(attended, w_out, preferred_element_type=jnp.float32), "head")
+    part = jnp.dot(attended, w_out, preferred_element_type=jnp.float32)
+    parts = lax.all_gather(part, "head", axis=0, tiled=False)
+    attn_sum = parts.sum(axis=0)
     resid = (hidden_in.astype(jnp.float32) + attn_sum).astype(jnp.bfloat16)
     moe_in = rms_scale(resid, moe_gain).astype(jnp.bfloat16)
     sigma = jax.nn.sigmoid(route_logits)

time: 327 us -> 313 us (0.957)
  waiting for transfers between devices: 39.9 us -> 18 us
  blocking collectives: 163 us -> 174 us
    psum x1 -> x0, waiting for transfers between devices: 25.5 us -> none  [shards(): lax.psum(jnp.dot(attended, w_out, preferred_element_type=jnp.float32), 'h...]
    all_gather x0 -> x1, blocking collectives: none -> 9.73 us  [shards(): parts = lax.all_gather(part, 'head', axis=0, tiled=False)]
  transfers between devices with their start and end apart: 5 -> 4, of which waited for: 2 -> 2; matrix products, arithmetic and copies ran while one was open for 8% -> 8% of each run, Pallas kernels for 0% -> 0%
where the time goes in v1:
time: 313 us; the launch traced here: 312 us
  blocking collectives  174 us (56%)
  local copies, waits for them, and re-layouts  42.2 us (13%)
  matrix products  30.3 us (10%)
  waiting for transfers between devices  18 us (6%)
  other arithmetic  17 us (5%)
  between operations  15.9 us (5%)
  starting transfers between devices  14.9 us (5%)
    unnamed x1, blocking collectives  69.5 us
    all_to_all x1, blocking collectives, shards(): lax.all_to_all(send_rows, 'blk', split_axis=0, concat_axis=0, tiled=True)  42.9 us
    all_gather x1, blocking collectives, shards(): lax.all_gather(queries.reshape(tok_rows, heads_here * (NOPE + ROPE)), 'bl...  27 us
    all_gather x1, blocking collectives, shards(): lax.all_gather(draft_rows[chosen], 'blk', axis=0, tiled=True)  19.8 us
    all_to_all x1, waiting for transfers between devices, shards(): lax.all_to_all(numer_out, 'blk', split_axis=0, concat_axis=0, tiled=True)  17.1 us
    all_gather x1, blocking collectives, shards(): parts = lax.all_gather(part, 'head', axis=0, tiled=False)  9.73 us
    dot_general x1, matrix products, shards(): jnp.einsum('sjcf,jfd->sjcd', act, w_down, preferred_element_type=jnp.floa...  8.3 us
    gather x2, local copies, waits for them, and re-layouts, shards(): back[slot_ids] * route_weight[:, None]  7.57 us
  transfers between devices with their start and end apart: 4, of which 2 were waited for; matrix products, arithmetic and copies ran while one was open for 8% of the time, Pallas kernels for 0%

profile of v1, /device:TPU:0, one launch (start us, length us, event | category | flops | bytes accessed | tf_op | source)
XLA Modules:
  0.0 311.9 jit_solution(7981610280791947897)
XLA Ops:
  10.8 2.0 fusion.53
  20.8 2.3 convolution_convert_fusion
  25.1 27.0 %all_gather.19 = bf16[512,768]{1,0:T(8,128)(2,1)} all-gather(bf16[32,768]{1,0:T(8,128)(2,1)} %convert_element_type.121), channel_id=1, replica_groups=mesh['head'=2,'blk'=16] {'blk'}, dimensions={0}, use_global_device_ids=true | all-gather | bytes 835584 | tf_op jit(solution)/shard_map/all_gather | solution.py:125
  52.2 3.4 %reshape.528 = bf16[16,32,4,192]{3,2,1,0:T(4,128)(2,1)} reshape(bf16[512,768]{1,0:T(8,128)(2,1)} %all_gather.19) | data formatting | bytes 1572864 | tf_op jit(solution)/shard_map/reshape | solution.py:142
  55.6 2.5 copy.84
  58.1 1.9 gather_fusion.1
  60.8 2.0 fusion.95
  63.8 3.5 %all-to-all-start.1 = ((f32[16,1,128]{2,1,0:T(1,128)}), f32[16,1,128]{2,1,0:T(1,128)S(1)}, u32[]{:S(2)}, u32[]{:S(2)}) async-start(f32[16,1,128]{2,1,0:T(1,128)} %reshape.623), calls=%async_computation.1 | async-start | bytes 16384 | tf_op jit(solution)/shard_map/all_to_all | solution.py:170
  68.7 1.7 convolution_bitcast_fusion.2
  70.5 4.8 %all-gather.3 = f32[2,288,32]{1,2,0:T(8,128)S(1)} all-gather(f32[1,288,32]{1,2,0:T(8,128)S(1)} %convolution_bitcast_fusion.2), channel_id=1, replica_groups=mesh['head'=2,'blk'=16] {'head'}, dimensions={0}, use_global_device_ids=true | all-gather | bytes 110592 | tf_op jit(solution)/shard_map/all_gather | solution.py:115
  77.1 2.3 convolution_convert_fusion.1
  79.4 1.8 reshape_reshape.4
  82.5 1.7 fusion.46
  84.8 2.7 copy.87
  87.5 2.6 all_to_all.22
  90.1 6.2 %all-to-all-start = ((f32[16,32,512]{2,1,0:T(8,128)}), f32[16,32,512]{2,1,0:T(8,128)}, u32[]{:S(2)}, u32[]{:S(2)}) async-start(f32[16,32,512]{2,1,0:T(8,128)} %all_to_all.22), calls=%async_computation | async-start | bytes 2097152 | tf_op jit(solution)/shard_map/all_to_all | solution.py:169
  102.2 17.1 %all-to-all-done = f32[16,32,512]{2,1,0:T(8,128)} async-done(((f32[16,32,512]{2,1,0:T(8,128)}), f32[16,32,512]{2,1,0:T(8,128)}, u32[]{:S(2)}, u32[]{:S(2)}) %all-to-all-start) | async-done | bytes 1048608 | tf_op jit(solution)/shard_map/all_to_all | solution.py:169
  120.7 2.0 fusion.56
  122.7 9.7 %all-gather = f32[64,2048]{1,0:T(8,128)} all-gather(f32[32,2048]{1,0:T(8,128)S(1)} %fusion.56), channel_id=2, replica_groups=mesh['head'=2,'blk'=16] {'head'}, dimensions={0}, use_global_device_ids=true | all-gather | bytes 786432 | tf_op jit(solution)/shard_map/all_gather | solution.py:193
  132.5 1.8 reduce_sum.117
  135.5 3.1 %gather_fusion.2 = bf16[384,2048]{1,0:T(8,128)(2,1)} fusion(bf16[33,2048]{1,0:T(8,128)(2,1)S(1)} %concatenate.30, s32[1024]{0:T(1024)S(1)} %pad_clamp_fusion.2), kind=kCustom, calls=%fused_computation.2 | custom fusion | bytes 3147264 | tf_op jit(solution)/shard_map/gather | solution.py:214
  138.6 42.9 %all_to_all.33 = bf16[16,24,2048]{2,1,0:T(8,128)(2,1)S(1)} all-to-all(bf16[16,24,2048]{2,1,0:T(8,128)(2,1)} %bitcast.172), channel_id=1, replica_groups=mesh['head'=2,'blk'=16] {'blk'}, dimensions={0} | all-to-all | bytes 3145728 | tf_op jit(solution)/shard_map/all_to_all | solution.py:215
  182.7 2.6 fusion.6
  185.2 8.3 %fusion = f32[16,24,2048]{2,1,0:T(8,128)} fusion(bf16[1,704,2048]{2,1,0:T(8,128)(2,1)} %param.41, bf16[16,24,2048]{2,1,0:T(8,128)(2,1)} %copy-done.3, bf16[1,704,2048]{2,1,0:T(8,128)(2,1)} %param.40, f32[16,1,24,704]{3,2,0,1:T(8,128)} %fusion.6), kind=kOutput, calls=%fused_computation.7 | convolution fusion | flops 2216214528 | bytes 11567104 | tf_op jit(solution)/shard_map/sjcf,jfd->sjcd/dot_general | solution.py:220
  193.5 5.2 %all-to-all-start.3 = ((f32[16,24,2048]{2,1,0:T(8,128)}), f32[16,24,2048]{2,1,0:T(8,128)}, u32[]{:S(2)}, u32[]{:S(2)}) async-start(f32[16,24,2048]{2,1,0:T(8,128)} %fusion), calls=%async_computation.3 | async-start | bytes 6291456 | tf_op jit(solution)/shard_map/all_to_all | solution.py:223
  201.0 69.5 %all-reduce.2 = s32[128]{0:T(128)S(1)} all-reduce(s32[128]{0:T(128)S(1)} %bitcast_dynamic-update-slice_fusion), channel_id=3, replica_groups=mesh['head'=2,'blk'=16] {'blk'}, use_global_device_ids=true, to_apply=%add.2 | all-reduce | flops 128 | bytes 1024
  270.5 4.9 %gather_fusion.3 = f32[192,2048]{1,0:T(8,128)} fusion(f32[384,2048]{1,0:T(8,128)} %bitcast.38, s32[1024]{0:T(1024)S(1)} %pad_clamp_fusion.1), kind=kCustom, calls=%fused_computation.3 | custom fusion | bytes 3146496 | tf_op jit(solution)/shard_map/gather | solution.py:225
  275.4 2.7 gather.21
  278.1 3.1 multiply_reduce_fusion
  281.2 19.8 %all-gather.2 = bf16[128,576]{1,0:T(8,128)(2,1)S(1)} all-gather(bf16[8,576]{1,0:T(8,128)(2,1)S(1)} %gather_fusion.4), channel_id=4, replica_groups=mesh['head'=2,'blk'=16] {'blk'}, dimensions={0}, use_global_device_ids=true | all-gather | bytes 156672 | tf_op jit(solution)/shard_map/all_gather | solution.py:128
  301.0 1.6 scatter_custom_fusion.1
  303.5 1.6 fusion.45
  (152 shorter events, 31.6 us)
Async XLA Ops:
  7.2 3.6 %copy-start = (bf16[768,2048]{1,0:T(8,128)(2,1)S(1)}, bf16[768,2048]{1,0:T(8,128)(2,1)}, u32[]{:S(2)}) copy-start(bf16[768,2048]{1,0:T(8,128)(2,1)} %param.23) | copy-start | bytes 9437188
  10.2 0.6 copy-start.18
  10.8 2.3 copy-start.1
  10.8 3.5 %copy-start.23 = (s32[3]{0:T(128)S(1)}, s32[3]{0:T(128)}, u32[]{:S(2)}) copy-start(s32[3]{0:T(128)} %param.31) | copy-start | bytes 40
  10.8 5.3 %copy-start.21 = (s32[1,32]{1,0:T(1,128)S(1)}, s32[1,32]{1,0:T(1,128)}, u32[]{:S(2)}) copy-start(s32[1,32]{1,0:T(1,128)} %param.33) | copy-start | bytes 388
  14.9 4.4 %copy-start.11 = (s32[1024]{0:T(1024)}, s32[1024]{0:T(1024)S(1)}, u32[]{:S(2)}) copy-start(s32[1024]{0:T(1024)S(1)} %pad_clamp_fusion.3) | copy-start | bytes 12292
  18.7 0.6 copy-start.12
  18.7 0.6 copy-start.14
  19.4 0.6 copy-start.4
  55.6 4.4 %copy-start.17 = (s32[3]{0:T(128)S(1)}, s32[3]{0:T(128)}, u32[]{:S(2)}) copy-start(s32[3]{0:T(128)} %gather_fusion) | copy-start | bytes 40
  55.6 5.2 %copy-start.6 = (bf16[3,128,64]{1,2,0:T(8,128)(2,1)S(1)}, bf16[3,128,64]{1,2,0:T(8,128)(2,1)}, u32[]{:S(2)}) copy-start(bf16[3,128,64]{1,2,0:T(8,128)(2,1)} %copy_bitcast_fusion) | copy-start | bytes 147460
  55.6 7.2 %copy-start.19 = (s32[3]{0:T(128)S(1)}, s32[3]{0:T(128)}, u32[]{:S(2)}) copy-start(s32[3]{0:T(128)} %param.30) | copy-start | bytes 40
  58.1 10.7 %copy-start.2 = (bf16[32,2048]{1,0:T(8,128)(2,1)S(1)}, bf16[32,2048]{1,0:T(8,128)(2,1)}, u32[]{:S(2)}) copy-start(bf16[32,2048]{1,0:T(8,128)(2,1)} %param.21) | copy-start | bytes 393220
  58.1 10.7 %copy-start.7 = (f32[2048]{0:T(1024)S(1)}, f32[2048]{0:T(1024)}, u32[]{:S(2)}) copy-start(f32[2048]{0:T(1024)} %param.22) | copy-start | bytes 24580
  60.8 14.9 %copy-start.16 = (f32[512]{0:T(512)S(1)}, f32[512]{0:T(512)}, u32[]{:S(2)}) copy-start(f32[512]{0:T(512)} %param.25) | copy-start | bytes 6148
  63.8 26.3 %all-to-all-start.1 = ((f32[16,1,128]{2,1,0:T(1,128)}), f32[16,1,128]{2,1,0:T(1,128)S(1)}, u32[]{:S(2)}, u32[]{:S(2)}) async-start(f32[16,1,128]{2,1,0:T(1,128)} %reshape.623), calls=%async_computation.1 | async-start | bytes 16384 | tf_op jit(solution)/shard_map/all_to_all | solution.py:170
  77.0 5.4 %copy-start.20 = (s32[3]{0:T(128)S(1)}, s32[3]{0:T(128)}, u32[]{:S(2)}) copy-start(s32[3]{0:T(128)} %param.30) | copy-start | bytes 40
  90.1 6.7 %copy-start.13 = (f32[32]{0:T(128)S(1)}, f32[32]{0:T(128)}, u32[]{:S(2)}) copy-start(f32[32]{0:T(128)} %copy-done.12) | copy-start | bytes 388
  90.1 6.7 %copy-start.15 = (f32[32]{0:T(128)S(1)}, f32[32]{0:T(128)}, u32[]{:S(2)}) copy-start(f32[32]{0:T(128)} %copy-done.14) | copy-start | bytes 388
  90.1 8.2 %copy-start.5 = (bf16[32,4,192]{2,0,1:T(8,128)(2,1)S(1)}, bf16[32,4,192]{2,0,1:T(8,128)(2,1)}, u32[]{:S(2)}) copy-start(bf16[32,4,192]{2,0,1:T(8,128)(2,1)} %copy-done.4) | copy-start | bytes 147460
  90.1 8.4 %copy-start.8 = (f32[16,1,128]{2,1,0:T(1,128)}, f32[16,1,128]{2,1,0:T(1,128)S(1)}, u32[]{:S(2)}) copy-start(f32[16,1,128]{2,1,0:T(1,128)S(1)} %all-to-all-done.1) | copy-start | bytes 24580
  90.1 29.2 %all-to-all-start = ((f32[16,32,512]{2,1,0:T(8,128)}), f32[16,32,512]{2,1,0:T(8,128)}, u32[]{:S(2)}, u32[]{:S(2)}) async-start(f32[16,32,512]{2,1,0:T(8,128)} %all_to_all.22), calls=%async_computation | async-start | bytes 2097152 | tf_op jit(solution)/shard_map/all_to_all | solution.py:169
  122.7 12.6 %copy-start.10 = (f32[2048]{0:T(1024)S(1)}, f32[2048]{0:T(1024)}, u32[]{:S(2)}) copy-start(f32[2048]{0:T(1024)} %param.36) | copy-start | bytes 24580
  138.6 44.0 %copy-start.22 = (bf16[1,704,2048]{2,1,0:T(8,128)(2,1)S(1)}, bf16[1,704,2048]{2,1,0:T(8,128)(2,1)}, u32[]{:S(2)}) copy-start(bf16[1,704,2048]{2,1,0:T(8,128)(2,1)} %param.39) | copy-start | bytes 8650756
  181.5 1.1 copy-start.3
  193.5 5.3 %copy-start.9 = (f32[32,6]{0,1:T(8,128)S(1)}, f32[32,6]{0,1:T(8,128)}, u32[]{:S(2)}) copy-start(f32[32,6]{0,1:T(8,128)} %param.38) | copy-start | bytes 2308
  193.5 5.4 %copy-start.26 = (u32[32]{0:T(128)S(1)}, u32[32]{0:T(128)}, u32[]{:S(2)}) copy-start(u32[32]{0:T(128)} %constant.93) | copy-start | bytes 388
  193.5 6.7 %copy-start.24 = (s32[1,8]{1,0:T(1,128)S(1)}, s32[1,8]{1,0:T(1,128)}, u32[]{:S(2)}) copy-start(s32[1,8]{1,0:T(1,128)} %param.34) | copy-start | bytes 100
  193.5 7.3 %copy-start.25 = (s32[1,8]{1,0:T(1,128)S(1)}, s32[1,8]{1,0:T(1,128)}, u32[]{:S(2)}) copy-start(s32[1,8]{1,0:T(1,128)} %param.35) | copy-start | bytes 100
  193.5 77.0 %all-to-all-start.3 = ((f32[16,24,2048]{2,1,0:T(8,128)}), f32[16,24,2048]{2,1,0:T(8,128)}, u32[]{:S(2)}, u32[]{:S(2)}) async-start(f32[16,24,2048]{2,1,0:T(8,128)} %fusion), calls=%async_computation.3 | async-start | bytes 6291456 | tf_op jit(solution)/shard_map/all_to_all | solution.py:223
  198.8 104.7 %all-reduce.5.cloned.1.call-start = ((), (), s32[]{:S(2)}) async-start(), calls=%async_computation.4 | async-start | bytes 524288 | tf_op jit(solution)/shard_map/psum | solution.py:229
Sparse Core Ops, SparseCore 0:
  281.3 22.1 all-reduce.4
